TPU v7x, 32 devices: a whole 2x2x4 slice. The times are simulated.
32 devices in a mesh: group: 2 (over core), ctx: 4 (over y, x), tp: 4 (over z).
Axes of the slice: x: 2, y: 2, z: 4, core: 2. Of those that a mesh axis runs over, the one named last changes fastest.
Arguments:
- activations: bfloat16 [1024, 8192], P(('group', 'ctx')), may hold values from -6 to 6
- queries: bfloat16 [1024, 4096], P(('group', 'ctx'), 'tp'), may hold values from -400 to 400
- out_grad: bfloat16 [1024, 4096], P(('group', 'ctx'), 'tp'), may hold values from -6 to 6
- key_weight: bfloat16 [8192, 512], P('ctx', 'tp'), may hold values from -0.0625 to 0.0625
- value_weight: bfloat16 [8192, 512], P('ctx', 'tp'), may hold values from -0.0625 to 0.0625
- sessions: int32 [4, 128], P('ctx'), may hold values from 0 to 3, never falling along the last dimension, each value on 1 to 64 neighbouring positions
Outputs:
- attention: bfloat16 [1024, 4096], P(('group', 'ctx'), 'tp')
- query_grad: bfloat16 [1024, 4096], P(('group', 'ctx'), 'tp')
- key_weight_grad: float32 [8192, 512], P(('group', 'ctx'), 'tp')
- value_weight_grad: float32 [8192, 512], P(('group', 'ctx'), 'tp')
- input_grad: bfloat16 [1024, 8192], P(('group', 'ctx'), 'tp')
Inputs may be any that keep to these rules, and one draw needn't show every extreme that they name: `sessions`: each row never falls; every session in a row has 1 to 64 tokens, and one session of each row has exactly that many.
All inputs are finite; a program needn't handle non-finite values.
Results may differ from a plain program's by a relative error of at most 0.025.
The roundings to bfloat16 on the way count: a program that leaves them out, or rounds other values in their place, can miss the bound.
Values may be sent and summed in bfloat16 or wider, within the bound.
A program may use at most 64 MiB of HBM per device.

v0:
```python
import math

import jax
import jax.numpy as jnp
from jax import lax
from jax.sharding import PartitionSpec as P

HQ = 32
KVH = 4
HD = 128


THETA = 500000.0


def rotate(vector, positions, turn_sign):
    half_dim = HD // 2
    frequency = THETA ** (-2.0 * jnp.arange(half_dim, dtype=jnp.float32) / HD)
    angles = positions.astype(jnp.float32)[:, None] * frequency[None, :]
    cosine = jnp.cos(angles)[:, None, :]
    sine_table = turn_sign * jnp.sin(angles)[:, None, :]
    shaped = vector.reshape(vector.shape[0], -1, HD)
    first_half = shaped[..., :half_dim]
    second_half = shaped[..., half_dim:]
    turned = jnp.concatenate(
        [
            first_half * cosine - second_half * sine_table,
            second_half * cosine + first_half * sine_table,
        ],
        -1,
    )
    return turned.reshape(vector.shape)


def body(activations, queries, out_grad, key_weight, value_weight, sessions):
    score_scale = 1.0 / math.sqrt(HD)
    tok_rows = activations.shape[0]
    ctx_count = lax.axis_size("ctx")
    total_rows = ctx_count * tok_rows
    key_block = min(total_rows, tok_rows * max(1, 512 // tok_rows))
    is_long = lax.axis_index("group") == 0
    own_first = lax.axis_index("ctx") * tok_rows
    local_rows = jnp.arange(tok_rows, dtype=jnp.int32)
    query_rows = own_first + local_rows
    positions = jnp.where(is_long, query_rows, local_rows)
    own_sessions = sessions[0]
    kv_cols = key_weight.shape[1]
    kv_heads = kv_cols // HD
    group_heads = HQ // KVH
    both_weights = jnp.concatenate([key_weight, value_weight], 1)
    whole_weights = lax.all_gather(both_weights, "ctx", axis=0, tiled=True)
    projected = jnp.dot(activations, whole_weights, preferred_element_type=jnp.float32)
    rotated_keys = rotate(projected[:, :kv_cols], positions, 1.0).astype(jnp.bfloat16)
    value_rows = projected[:, kv_cols:].astype(jnp.bfloat16)
    rotated = rotate(queries.astype(jnp.float32), positions, 1.0).astype(jnp.bfloat16)
    query_heads = rotated.reshape(tok_rows, kv_heads, group_heads, HD)
    grad_heads = out_grad.reshape(tok_rows, kv_heads, group_heads, HD)
    context = lax.all_gather(
        jnp.concatenate([rotated_keys, value_rows], 1), "ctx", axis=0, tiled=True
    )
    first_block = jnp.where(is_long, 0, own_first // key_block)
    stop_block = own_first // key_block + 1

    def block_scores(block_index):
        block_first = (block_index * key_block).astype(jnp.int32)
        block_kv = lax.dynamic_slice_in_dim(context, block_first, key_block, 0)
        block_keys = block_kv[:, :kv_cols].reshape(key_block, kv_heads, HD)
        block_values = block_kv[:, kv_cols:].reshape(key_block, kv_heads, HD)
        key_rows = block_first + jnp.arange(key_block, dtype=jnp.int32)
        key_sessions = lax.dynamic_update_slice(
            jnp.full((key_block,), -1, jnp.int32), own_sessions, (own_first - block_first,)
        )
        same_session = own_sessions[:, None] == key_sessions[None, :]
        allowed = (key_rows[None, :] <= query_rows[:, None]) & (is_long | same_session)
        scores = (
            jnp.einsum(
                "qkgd,skd->kgqs", query_heads, block_keys, preferred_element_type=jnp.float32
            )
            * score_scale
        )
        scores = jnp.where(allowed[None, None], scores, -jnp.inf)
        return (scores, block_keys, block_values, block_first)

    def max_pass(block_index, loop_state):
        running_max, running_sum = loop_state
        scores = block_scores(block_index)[0]
        new_max = jnp.maximum(running_max, jnp.max(scores, -1))
        running_sum = running_sum * jnp.exp(running_max - new_max) + jnp.sum(
            jnp.exp(scores - new_max[..., None]), -1
        )
        return (new_max, running_sum)

    stat_shape = (kv_heads, group_heads, tok_rows)
    row_max, row_total = lax.fori_loop(
        first_block,
        stop_block,
        max_pass,
        (jnp.full(stat_shape, -jnp.inf, jnp.float32), jnp.zeros(stat_shape, jnp.float32)),
    )
    log_total = row_max + jnp.log(row_total)

    def output_pass(block_index, running):
        scores, block_keys, block_values, block_first = block_scores(block_index)
        rounded_weights = jnp.exp(scores - log_total[..., None]).astype(jnp.bfloat16)
        return running + jnp.einsum(
            "kgqs,skd->qkgd", rounded_weights, block_values, preferred_element_type=jnp.float32
        )

    attended = lax.fori_loop(
        first_block,
        stop_block,
        output_pass,
        jnp.zeros((tok_rows, kv_heads, group_heads, HD), jnp.float32),
    )
    attention = attended.reshape(tok_rows, kv_heads * group_heads * HD).astype(jnp.bfloat16)
    out_dot = jnp.einsum(
        "qkgd,qkgd->kgq",
        grad_heads.astype(jnp.float32),
        attention.astype(jnp.float32).reshape(tok_rows, kv_heads, group_heads, HD),
    )

    def grad_pass(block_index, loop_state):
        query_acc, key_buffer = loop_state
        scores, block_keys, block_values, block_first = block_scores(block_index)
        weights = jnp.exp(scores - log_total[..., None])
        rounded_weights = weights.astype(jnp.bfloat16)
        prob_grad = jnp.einsum(
            "qkgd,skd->kgqs", grad_heads, block_values, preferred_element_type=jnp.float32
        )
        score_grad = (weights * (prob_grad - out_dot[..., None])).astype(jnp.bfloat16)
        query_acc = query_acc + jnp.einsum(
            "kgqs,skd->qkgd", score_grad, block_keys, preferred_element_type=jnp.float32
        )
        key_part = (
            jnp.einsum(
                "kgqs,qkgd->skd", score_grad, query_heads, preferred_element_type=jnp.float32
            )
            * score_scale
        )
        value_part = jnp.einsum(
            "kgqs,qkgd->skd", rounded_weights, grad_heads, preferred_element_type=jnp.float32
        )
        update = jnp.concatenate(
            [key_part.reshape(key_block, kv_cols), value_part.reshape(key_block, kv_cols)], 1
        )
        key_buffer = lax.dynamic_update_slice(key_buffer, update, (block_first, jnp.int32(0)))
        return (query_acc, key_buffer)

    query_acc, key_buffer = lax.fori_loop(
        first_block,
        stop_block,
        grad_pass,
        (
            jnp.zeros((tok_rows, kv_heads, group_heads, HD), jnp.float32),
            jnp.zeros((total_rows, 2 * kv_cols), jnp.float32),
        ),
    )
    query_grad = rotate(
        query_acc.reshape(tok_rows, kv_heads * group_heads * HD) * score_scale, positions, -1.0
    ).astype(jnp.bfloat16)
    summed = lax.psum_scatter(key_buffer, "ctx", scatter_dimension=0, tiled=True)
    key_grad = rotate(summed[:, :kv_cols], positions, -1.0).astype(jnp.bfloat16)
    value_grad = summed[:, kv_cols:].astype(jnp.bfloat16)
    kv_grads = jnp.concatenate([key_grad, value_grad], 1)
    input_terms = lax.dot_general(
        kv_grads, whole_weights, (((1,), (1,)), ((), ())), preferred_element_type=jnp.float32
    )
    input_grad = lax.psum_scatter(input_terms, "tp", scatter_dimension=1, tiled=True).astype(
        jnp.bfloat16
    )
    column_rows = lax.all_to_all(
        activations, ("group", "ctx"), split_axis=1, concat_axis=0, tiled=True
    )
    owned_rows = lax.dot_general(
        column_rows,
        lax.all_gather(kv_grads, ("group", "ctx"), axis=0, tiled=True),
        (((0,), (0,)), ((), ())),
        preferred_element_type=jnp.float32,
    )
    key_weight_grad = owned_rows[:, :kv_cols]
    value_weight_grad = owned_rows[:, kv_cols:]
    return (attention, query_grad, key_weight_grad, value_weight_grad, input_grad)


def solution(mesh):
    placed = (
        P(("group", "ctx"), None),
        P(("group", "ctx"), "tp"),
        P(("group", "ctx"), "tp"),
        P("ctx", "tp"),
        P("ctx", "tp"),
        P("ctx", None),
    )
    return jax.shard_map(
        body,
        mesh=mesh,
        in_specs=placed,
        out_specs=(
            P(("group", "ctx"), "tp"),
            P(("group", "ctx"), "tp"),
            P(("group", "ctx"), "tp"),
            P(("group", "ctx"), "tp"),
            P(("group", "ctx"), "tp"),
        ),
        check_vma=False,
    )
```

profile of v0, /device:TPU:0, one launch (start us, length us, event | category | flops | bytes accessed | tf_op | source)
XLA Modules:
  0.0 210.1 jit_solution(12914593772049069902)
XLA Ops:
  7.2 2.3 %pad_maximum_fusion.1 = bf16[2048,256]{1,0:T(8,128)(2,1)} fusion(bf16[2048,128]{1,0:T(8,128)(2,1)} %param.16, bf16[2048,128]{1,0:T(8,128)(2,1)} %param.15), kind=kLoop, calls=%fused_computation.66 | loop fusion | flops 2097152 | bytes 2097152 | tf_op jit(solution)/shard_map/concatenate | solution.py:50
  9.9 0.2 broadcast_multiply_fusion
  10.2 0.2 copy.54
  10.7 0.8 copy.78
  11.4 53.9 %all-gather.2.cloned.1.call-done = bf16[8192,256]{1,0:T(8,128)(2,1)} async-done(((bf16[2048,256]{1,0:T(8,128)(2,1)}), bf16[8192,256]{1,0:T(8,128)(2,1)}) %all-gather.2.cloned.1.call-update) | async-done | bytes 4194320 | tf_op jit(solution)/shard_map/all_gather | solution.py:51
  65.3 3.5 %convolution_bitcast_fusion.5 = f32[128,256]{0,1:T(8,128)S(1)} fusion(bf16[8192,256]{1,0:T(8,128)(2,1)} %all-gather.2.cloned.1.call-done, bf16[128,8192]{1,0:T(8,128)(2,1)S(1)} %copy-done), kind=kOutput, calls=%fused_computation.65 | convolution fusion | flops 536870912 | bytes 6422528 | tf_op jit(solution)/shard_map/dot_general | solution.py:52
  68.8 0.2 fusion.65
  69.0 8.9 %all_gather.10 = bf16[512,256]{0,1:T(8,128)(2,1)S(1)} all-gather(bf16[128,256]{0,1:T(8,128)(2,1)S(1)} %pad_maximum_fusion.4), channel_id=1, replica_groups=mesh['group'=2,'ctx'=4,'tp'=4] {'ctx'}, dimensions={0}, use_global_device_ids=true | all-gather | bytes 327680 | tf_op jit(solution)/shard_map/all_gather | solution.py:58
  78.2 1.5 while.40
  78.2 0.2 dynamic_update_slice.59
  78.5 0.2 or_and_fusion.6
  78.7 0.4 fusion.97
  79.2 0.4 exponential_reduce_fusion.2
  79.6 0.6 log_add_fusion
  80.2 0.8 broadcast.346.clone
  81.1 3.2 %while.41 = (s32[]{:T(128)}, f32[128,1,8,128]{3,0,2,1:T(8,128)}, s32[]{:T(128)}, pred[]{:T(512)}, s32[1,128]{1,0:T(1,128)S(1)}, /*index=5*/s32[]{:T(128)}, s32[1...) while((s32[]{:T(128)}, f32[128,1,8,128]{3,0,2,1:T(8,128)}, ...), condition=%wide.region_5.6_spmd.clone.clone, body=%wide.region_4.5_spmd.clone.clone.sunk | while | flops 270926464 | bytes 1718992 | solution.py:109
  81.1 0.2 dynamic_update_slice.61
  81.3 0.2 or_and_fusion.7
  81.6 2.8 %fusion.101 = f32[128,1,8,128]{3,0,2,1:T(8,128)} fusion(f32[128,1,8,128]{3,0,2,1:T(8,128)} %get-tuple-element.823, f32[8,128]{1,0:T(8,128)} %bitcast.218, pred[128,512]{0,1:T(8,128)(4,1)S(1)} %or_and_fusion.7, bf16[128,1,8,128]{3,0,2,1:T(8,128)(2,1)S(1)} %get-tuple-element.844, bf16[512,256]{1,0:T(8,128)(2,1)S(1)} %get-tuple-element.843), kind=kOutput, calls=%fused_computation.21.clone.1 | convolution fusion | flops 270663680 | bytes 1642496 | tf_op jit(solution)/shard_map/while/body/kgqs,skd->qkgd/dot_general | solution.py:105
  84.3 1.8 bitcast_convert_fusion
  86.1 0.4 multiply_reduce_fusion
  86.6 0.9 broadcast_in_dim.52
  87.5 4.5 %while.42 = (s32[]{:T(128)}, f32[128,1,8,128]{3,0,2,1:T(8,128)S(1)}, f32[512,256]{0,1:T(8,128)}, s32[]{:T(128)}, pred[]{:T(512)}, /*index=5*/s32[1,128]{1,0:T(1,...) while((s32[]{:T(128)}, ...), condition=%wide.region_7.8_spmd.clone.clone, body=%wide.region_6.7_spmd.clone.clone.sunk | while | flops 675349120 | bytes 13650664 | solution.py:149
  87.6 0.2 dynamic_update_slice.63
  87.8 0.2 or_and_fusion.8
  88.0 1.2 fusion.112
  89.3 0.5 convolution_bitcast_fusion.7
  89.8 0.4 fusion.113
  90.2 0.5 fusion.115
  90.7 0.5 fusion.114
  91.2 0.8 pad_maximum_fusion.8
  92.1 24.9 %reduce-scatter.3.cloned.1.call-done = f32[128,256]{0,1:T(8,128)} async-done(((f32[512,256]{0,1:T(8,128)}), f32[128,256]{0,1:T(8,128)}) %reduce-scatter.3.cloned.1.call-update) | async-done | bytes 131088 | tf_op jit(solution)/shard_map/reduce_scatter | solution.py:161
  117.0 0.8 slice_bitcast_fusion
  117.9 0.2 fusion.61
  118.1 0.8 slice.150
  118.9 5.6 %fusion.69 = f32[128,8192]{1,0:T(8,128)} fusion(bf16[8192,256]{1,0:T(8,128)(2,1)} %all-gather.2.cloned.1.call-done, bf16[128,128]{0,1:T(8,128)(2,1)S(1)} %slice.150, bf16[128,128]{0,1:T(8,128)(2,1)S(1)} %maximum_bitcast_fusion.1), kind=kOutput, calls=%fused_computation.113 | convolution fusion | flops 537001984 | bytes 8454144 | tf_op jit(solution)/shard_map/dot_general | solution.py:165
  124.6 2.5 %copy.59 = bf16[128,8192]{0,1:T(8,128)(2,1)} copy(bf16[128,8192]{1,0:T(8,128)(2,1)S(1)} %copy-done) | data formatting | bytes 4194304 | tf_op args[0]
  127.1 30.6 %all_to_all.19 = bf16[128,8,1024]{0,2,1:T(8,128)(2,1)} all-to-all(bf16[128,8,1024]{0,2,1:T(8,128)(2,1)} %bitcast.242), channel_id=1, replica_groups=mesh['group'=2,'ctx'=4,'tp'=4] {'group','ctx'}, dimensions={1} | all-to-all | bytes 4194304 | tf_op jit(solution)/shard_map/all_to_all | solution.py:171
  157.6 2.9 %copy.60 = bf16[8,128,1024]{2,1,0:T(8,128)(2,1)S(1)} copy(bf16[8,128,1024]{1,2,0:T(8,128)(2,1)} %bitcast.241) | data formatting | bytes 4194304 | tf_op jit(solution)/shard_map/all_to_all | solution.py:171
  160.7 0.8 copy.81
  161.5 0.2 copy.58
  161.9 0.9 copy.61
  162.7 22.4 %all_gather.11 = bf16[1024,256]{0,1:T(8,128)(2,1)S(1)} all-gather(bf16[128,256]{0,1:T(8,128)(2,1)S(1)} %pad_maximum_fusion.5), channel_id=1, replica_groups=mesh['group'=2,'ctx'=4,'tp'=4] {'group','ctx'}, dimensions={0}, use_global_device_ids=true | all-gather | bytes 589824 | tf_op jit(solution)/shard_map/all_gather | solution.py:176
  185.1 0.7 convolution_bitcast_fusion.4
  185.9 1.0 copy.63
  186.9 1.0 copy.62
  187.9 13.6 %reduce-scatter.5.cloned.1.call-done = f32[128,2048]{1,0:T(8,128)} async-done(((f32[128,8192]{1,0:T(8,128)}), f32[128,2048]{1,0:T(8,128)}) %reduce-scatter.5.cloned.1.call-update) | async-done | bytes 1048592 | tf_op jit(solution)/shard_map/reduce_scatter | solution.py:168
  201.5 2.1 convert_element_type.60
  (61 shorter events, 1.5 us)
Async XLA Ops:
  7.2 2.5 %copy-start.4 = (bf16[128,1024]{1,0:T(8,128)(2,1)S(1)}, bf16[128,1024]{1,0:T(8,128)(2,1)}, u32[]{:S(2)}) copy-start(bf16[128,1024]{1,0:T(8,128)(2,1)} %param.13) | copy-start | bytes 786436
  7.2 58.1 %all-gather.2.cloned.1.call-start = ((), (), s32[]{:S(2)}) async-start(), calls=%async_computation.3 | async-start | bytes 5242880 | tf_op jit(solution)/shard_map/all_gather | solution.py:51
  9.5 0.9 copy-start.2
  9.6 107.4 %reduce-scatter.3.cloned.1.call-start = ((), (), s32[]{:S(2)}) async-start(), calls=%async_computation.4 | async-start | bytes 655360 | tf_op jit(solution)/shard_map/reduce_scatter | solution.py:161
  9.6 55.6 %copy-start = (bf16[128,8192]{1,0:T(8,128)(2,1)S(1)}, bf16[128,8192]{1,0:T(8,128)(2,1)}, u32[]{:S(2)}) copy-start(bf16[128,8192]{1,0:T(8,128)(2,1)} %param.12) | copy-start | bytes 6291460
  9.9 58.9 %copy-start.6 = (f32[128]{0:T(128)}, f32[128]{0:T(128)S(1)}, u32[]{:S(2)}) copy-start(f32[128]{0:T(128)S(1)} %fusion.68) | copy-start | bytes 1540
  9.9 58.9 %copy-start.8 = (f32[64]{0:T(128)}, f32[64]{0:T(128)S(1)}, u32[]{:S(2)}) copy-start(f32[64]{0:T(128)S(1)} %multiply_power_fusion) | copy-start | bytes 772
  11.4 66.7 %copy-start.5 = (s32[1,128]{1,0:T(1,128)S(1)}, s32[1,128]{1,0:T(1,128)}, u32[]{:S(2)}) copy-start(s32[1,128]{1,0:T(1,128)} %param.17) | copy-start | bytes 1540
  81.1 5.1 %copy-start.3 = (bf16[16,8,8,128]{3,2,1,0:T(8,128)(2,1)S(1)}, bf16[16,8,8,128]{3,2,1,0:T(8,128)(2,1)}, u32[]{:S(2)}) copy-start(bf16[16,8,8,128]{3,2,1,0:T(8,128)(2,1)} %copy.78) | copy-start | bytes 786436
  87.5 30.4 %copy-start.7 = (f32[128]{0:T(128)S(1)}, f32[128]{0:T(128)}, u32[]{:S(2)}) copy-start(f32[128]{0:T(128)} %copy-done.6) | copy-start | bytes 1540
  87.5 30.3 %copy-start.9 = (f32[64]{0:T(128)S(1)}, f32[64]{0:T(128)}, u32[]{:S(2)}) copy-start(f32[64]{0:T(128)} %copy-done.8) | copy-start | bytes 772
  92.1 109.4 %reduce-scatter.5.cloned.1.call-start = ((), (), s32[]{:S(2)}) async-start(), calls=%async_computation.5 | async-start | bytes 5242880 | tf_op jit(solution)/shard_map/reduce_scatter | solution.py:168
  157.6 2.9 %copy-start.1 = (bf16[128,1,8,128]{3,0,2,1:T(8,128)(2,1)S(1)}, bf16[128,1,8,128]{3,0,2,1:T(8,128)(2,1)}, u32[]{:S(2)}) copy-start(bf16[128,1,8,128]{3,0,2,1:T(8,128)(2,1)} %get-tuple-element.544) | copy-start | bytes 786436
Sparse Core Ops, SparseCore 0:
  9.9 55.3 all-gather.1
  92.2 24.7 reduce-scatter.2
  124.7 76.7 reduce-scatter.4
where the time goes:
time: 211 us; the launch traced here: 210 us
  waiting for transfers between devices  92.4 us (44%)
  blocking collectives  61.9 us (29%)
  matrix products  16.1 us (8%)
  local copies, waits for them, and re-layouts  15.2 us (7%)
  between operations  14.1 us (7%)
  other arithmetic  10.1 us (5%)
    all_gather x1, waiting for transfers between devices, body(): whole_weights = lax.all_gather(both_weights, 'ctx', axis=0, tiled=True)  53.9 us
    all_to_all x1, blocking collectives, body(): lax.all_to_all(activations, ('group', 'ctx'), split_axis=1, concat_axis=0...  30.6 us
    reduce_scatter x1, waiting for transfers between devices, body(): lax.psum_scatter(key_buffer, 'ctx', scatter_dimension=0, tiled=True)  24.9 us
    all_gather x1, blocking collectives, body(): lax.all_gather(kv_grads, ('group', 'ctx'), axis=0, tiled=True)  22.4 us
    reduce_scatter x1, waiting for transfers between devices, body(): lax.psum_scatter(input_terms, 'tp', scatter_dimension=1, tiled=True)  13.6 us
    all_gather x1, blocking collectives, body(): lax.all_gather(jnp.concatenate([rotated_keys, value_rows], 1), 'ctx', axi...  8.95 us
    unnamed x30, local copies, waits for them, and re-layouts  7.56 us
    dot_general x1, matrix products, body(): lax.dot_general(kv_grads, whole_weights, (((1,), (1,)), ((), ())), prefer...  5.64 us
  transfers between devices with their start and end apart: 3, of which 3 were waited for; matrix products, arithmetic and copies ran while one was open for 6% of the time, Pallas kernels for 0%

commit v1 on v0

v1 whole, which is shorter than its diff:
```python
import functools
import math

import jax
import jax.numpy as jnp
from jax import lax
from jax.experimental import pallas as pl
from jax.experimental.pallas import tpu as pltpu
from jax.sharding import PartitionSpec as P

HD = 128
THETA = 500000.0
BF = jnp.bfloat16
F32 = jnp.float32
MESH = pl.DeviceIdType.MESH


def dot(a, b, dims):
    return lax.dot_general(a, b, (dims, ((), ())), preferred_element_type=F32)


def kernel(
    G, C, T,
    act_hbm, q_hbm, do_hbm, wk_hbm, wv_hbm, ses_hbm,
    att_ref, dq_ref, kwg_ref, vwg_ref, ig_ref,
    wall, w2, act, q_in, do_in, ses, arecv, qs, dos, kv, scores, dkv, grecv,
    kvg, kvg_tp, cos_ref, sin_ref, proj, dq_acc,
    loc, w_s, w_r, sb_s, sb_r, z_s, z_r, zf_s, zf_r, a_s, a_r, k_s, k_r,
    d_s, d_r, p_s, p_r, t_s, t_r,
):
    g = lax.axis_index("group")
    c = lax.axis_index("ctx")
    t = lax.axis_index("tp")
    R = act_hbm.shape[0]
    D = act_hbm.shape[1]
    WR = wk_hbm.shape[0]
    CR = min(WR, 512)
    NCH = WR // CR
    DB = D // (G * C)
    DT = D // T
    NK = DT // CR
    H = q_hbm.shape[1] // HD
    scale = 1.0 / math.sqrt(HD)
    is_long = g == 0
    lanes = pl.ds(pl.multiple_of(g * HD, HD), HD)
    olanes = pl.ds(pl.multiple_of((1 - g) * HD, HD), HD)

    def remote(src, dst, ss, rs, **dev):
        return pltpu.make_async_remote_copy(
            src_ref=src, dst_ref=dst, send_sem=ss, recv_sem=rs, device_id=dev, device_id_type=MESH
        )

    def loop(n, f, first=0):
        def step(i, carry):
            f(i)
            return carry

        lax.fori_loop(first, n, step, 0)

    own_rows = pl.ds(pl.multiple_of(c * WR, WR), WR)
    locals_ = [
        pltpu.make_async_copy(wk_hbm, wall.at[own_rows, pl.ds(0, HD)], loc.at[0]),
        pltpu.make_async_copy(wv_hbm, wall.at[own_rows, pl.ds(HD, HD)], loc.at[1]),
        pltpu.make_async_copy(act_hbm, act, loc.at[2]),
        pltpu.make_async_copy(q_hbm, q_in, loc.at[3]),
        pltpu.make_async_copy(do_hbm, do_in, loc.at[4]),
        pltpu.make_async_copy(ses_hbm, ses, loc.at[5]),
    ]
    for one in locals_:
        one.start()

    barrier = pltpu.get_barrier_semaphore()
    me = g * C + c

    def greet_plane(i):
        b = lax.rem(me + i, G * C)
        pl.semaphore_signal(
            barrier, inc=1, device_id={"group": b // C, "ctx": lax.rem(b, C)}, device_id_type=MESH
        )

    def greet_tp(i):
        pl.semaphore_signal(
            barrier, inc=1, device_id={"tp": lax.rem(t + i, T)}, device_id_type=MESH
        )

    loop(G * C, greet_plane, 1)
    loop(T, greet_tp, 1)
    pl.semaphore_wait(barrier, G * C - 1 + T - 1)
    locals_[0].wait()
    locals_[1].wait()

    def rows_of(owner, ch):
        return pl.ds(pl.multiple_of(owner * WR + ch * CR, CR), CR)

    def w_copy(owner, ch, d):
        place = wall.at[rows_of(owner, ch), lanes]
        return remote(
            place, place, w_s.at[d, ch], w_r.at[owner, ch], ctx=lax.rem(c + d, C)
        )

    def send_w(i):
        w_copy(c, i // (C - 1), lax.rem(i, C - 1) + 1).start()

    loop(NCH * (C - 1), send_w)

    def sib_copy(owner, ch, which):
        place = wall.at[rows_of(owner, ch), which]
        return remote(place, place, sb_s.at[owner, ch], sb_r.at[owner, ch], group=1 - g)

    def z_target(owner, ch):
        first = owner * WR + ch * CR
        return first // DT, lax.rem(first, DT) // CR

    def z_start(owner, ch):
        to, piece = z_target(owner, ch)

        @pl.when(to != t)
        def _():
            z_copy(owner, ch, to, t, piece).start()

    def z_copy(owner, ch, to, head, piece):
        return remote(
            wall.at[rows_of(owner, ch), lanes],
            w2.at[head, pl.ds(pl.multiple_of(piece * CR, CR), CR), lanes],
            z_s.at[owner, ch], z_r.at[head, piece], tp=to,
        )

    def own_z(ch):
        z_start(c, ch)

    loop(NCH, own_z)

    lane = lax.broadcasted_iota(jnp.int32, (R, HD), 1)
    row = lax.broadcasted_iota(jnp.int32, (R, HD), 0)
    half = lax.rem(lane, HD // 2).astype(F32)
    freq = jnp.exp(half * (-2.0 * math.log(THETA) / HD))
    angle = (row + jnp.where(is_long, c * R, 0)).astype(F32) * freq
    cos_ref[...] = jnp.cos(angle)
    sin_ref[...] = jnp.where(lane < HD // 2, -1.0, 1.0) * jnp.sin(angle)

    def rope(u, sign):
        return u * cos_ref[...] + pltpu.roll(u, HD // 2, 1) * (sin_ref[...] * sign)

    for one in locals_[2:]:
        one.wait()
    for h in range(H):
        cols = slice(h * HD, (h + 1) * HD)
        qs[h] = rope(q_in[:, cols].astype(F32), 1.0).astype(BF)
        dos[h] = do_in[:, cols]

    proj[...] = jnp.zeros_like(proj)

    def project(owner, ch):
        first = pl.multiple_of(owner * WR + ch * CR, CR)
        proj[...] += dot(act[:, pl.ds(first, CR)], wall[rows_of(owner, ch), :], ((1,), (0,)))

    def own_project(ch):
        project(c, ch)

    loop(NCH, own_project)

    def arrived(i):
        ch = i // (C - 1)
        owner = lax.rem(c + C - (lax.rem(i, C - 1) + 1), C)
        w_copy(owner, ch, 1).wait_recv()
        sib_copy(owner, ch, lanes).start()
        z_start(owner, ch)

    def use(i):
        ch = i // (C - 1)
        owner = lax.rem(c + C - (lax.rem(i, C - 1) + 1), C)
        sib_copy(owner, ch, olanes).wait_recv()
        project(owner, ch)

    def chunk(ch):
        loop((ch + 1) * (C - 1), arrived, ch * (C - 1))

        @pl.when(ch > 0)
        def _():
            loop(ch * (C - 1), use, (ch - 1) * (C - 1))

    loop(NCH, chunk)

    def a_copy(i, slot):
        b = lax.rem(me + i, G * C)
        return remote(
            act.at[:, pl.ds(pl.multiple_of(b * DB, DB), DB)],
            arecv.at[pl.ds(pl.multiple_of(slot * R, R), R), :],
            a_s.at[i], a_r.at[slot],
            group=b // C, ctx=lax.rem(b, C),
        )

    def a_start(i):
        a_copy(i, me).start()

    loop(G * C, a_start, 1)
    own_a = pltpu.make_async_copy(
        act.at[:, pl.ds(pl.multiple_of(me * DB, DB), DB)],
        arecv.at[pl.ds(pl.multiple_of(me * R, R), R), :],
        loc.at[0],
    )
    own_a.start()
    loop(NCH * (C - 1), use, (NCH - 1) * (C - 1))

    kv[c, :, :HD] = rope(proj[:, :HD], 1.0).astype(BF)
    kv[c, :, HD:] = proj[:, HD:].astype(BF)

    def kv_copy(owner, to):
        return remote(kv.at[owner], kv.at[owner], k_s.at[to], k_r.at[owner], ctx=to)

    @pl.when(is_long)
    def _():
        loop(C, lambda to: kv_copy(c, to).start(), c + 1)

    first_block = jnp.where(is_long, 0, c)
    srow = jnp.broadcast_to(ses[...].astype(F32), (R, R))
    same = (srow == srow.T) | is_long
    q_pos = lax.broadcasted_iota(jnp.int32, (R, R), 0)
    k_pos = lax.broadcasted_iota(jnp.int32, (R, R), 1)
    queries = qs[...].reshape(H * R, HD)

    def score_pass(i, top):
        j = c - i + first_block * 0

        @pl.when(j != c)
        def _():
            kv_copy(j, 0).wait_recv()

        s = dot(queries, kv[j, :, :HD], ((1,), (1,))) * scale
        allowed = same & (k_pos <= q_pos + (c - j) * R)
        s = jnp.where(allowed[None], s.reshape(H, R, R), -jnp.inf).reshape(H * R, R)
        scores[j] = s
        return jnp.maximum(top, jnp.max(s, 1, keepdims=True))

    count = c + 1 - first_block
    top = lax.fori_loop(0, count, score_pass, jnp.full((H * R, 1), -jnp.inf, F32))

    def sum_pass(j, total):
        return total + jnp.sum(jnp.exp(scores[j] - top), 1, keepdims=True)

    total = lax.fori_loop(first_block, c + 1, sum_pass, jnp.zeros((H * R, 1), F32))
    log_total = top + jnp.log(total)

    dq_acc[...] = jnp.zeros_like(dq_acc)

    def out_pass(j):
        w = jnp.exp(scores[j] - log_total)
        scores[j] = w
        dq_acc[...] += dot(w.astype(BF), kv[j, :, HD:], ((1,), (0,)))

    loop(c + 1, out_pass, first_block)
    attended = dq_acc[...].astype(BF)
    for h in range(H):
        att_ref[:, h * HD:(h + 1) * HD] = attended[h * R:(h + 1) * R]
    grads = dos[...].reshape(H * R, HD)
    out_dot = jnp.sum(grads.astype(F32) * attended.astype(F32), 1, keepdims=True)
    dq_acc[...] = jnp.zeros_like(dq_acc)

    def d_copy(owner, source):
        return remote(dkv.at[owner], grecv.at[source], d_s.at[owner], d_r.at[source], ctx=owner)

    def grad_pass(j):
        w = scores[j]
        prob_grad = dot(grads, kv[j, :, HD:], ((1,), (1,)))
        ds = (w * (prob_grad - out_dot)).astype(BF)
        dkv[j, :, :HD] = dot(ds, queries, ((0,), (0,))) * scale
        dkv[j, :, HD:] = dot(w.astype(BF), grads, ((0,), (0,)))

        @pl.when(j != c)
        def _():
            d_copy(j, c).start()

        dq_acc[...] += dot(ds, kv[j, :, :HD], ((1,), (0,)))

    loop(c + 1, grad_pass, first_block)
    for h in range(H):
        turned = rope(dq_acc[h * R:(h + 1) * R] * scale, -1.0)
        dq_ref[:, h * HD:(h + 1) * HD] = turned.astype(BF)

    proj[...] = dkv[c]

    def add_grad(source):
        d_copy(0, source).wait_recv()
        proj[...] += grecv[source]

    @pl.when(is_long)
    def _():
        loop(C, add_grad, c + 1)

    my_rows = pl.ds(pl.multiple_of(me * R, R), R)
    kvg[my_rows, :HD] = rope(proj[:, :HD], -1.0).astype(BF)
    kvg[my_rows, HD:] = proj[:, HD:].astype(BF)

    def p_copy(i, slot):
        b = lax.rem(me + i, G * C)
        rows = pl.ds(pl.multiple_of(slot * R, R), R)
        return remote(
            kvg.at[rows], kvg.at[rows], p_s.at[i], p_r.at[slot], group=b // C, ctx=lax.rem(b, C)
        )

    def t_copy(i, slot):
        return remote(kvg.at[my_rows], kvg_tp.at[slot], t_s.at[i], t_r.at[slot], tp=lax.rem(t + i, T))

    loop(T, lambda i: t_copy(i, t).start(), 1)
    loop(G * C, lambda i: p_copy(i, me).start(), 1)

    def zf_copy(head, piece, which):
        place = w2.at[head, pl.ds(pl.multiple_of(piece * CR, CR), CR), which]
        return remote(place, place, zf_s.at[head, piece], zf_r.at[head, piece], group=1 - g)

    def z_arrived(i):
        head = lax.rem(t + 1 + i // NK, T)
        piece = lax.rem(i, NK)
        z_copy(0, 0, 0, head, piece).wait_recv()
        zf_copy(head, piece, lanes).start()

    loop((T - 1) * NK, z_arrived)

    own_a.wait()

    def a_wait(i):
        slot = lax.rem(me + i, G * C)
        a_copy(0, slot).wait_recv()
        p_copy(0, slot).wait_recv()

    loop(G * C, a_wait, 1)
    step = min(DB, 256)

    def wgrad(i):
        at = pl.ds(pl.multiple_of(i * step, step), step)
        both = dot(arecv[:, at], kvg[...], ((0,), (0,)))
        kwg_ref[at, :] = both[:, :HD]
        vwg_ref[at, :] = both[:, HD:]

    loop(DB // step, wgrad)

    loop(T, lambda i: t_copy(0, lax.rem(t + i, T)).wait_recv(), 1)

    def z_wait(i):
        zf_copy(lax.rem(t + 1 + i // NK, T), lax.rem(i, NK), olanes).wait_recv()

    loop((T - 1) * NK, z_wait)

    def igrad(i):
        at = pl.multiple_of(i * CR, CR)
        own = wall[pl.ds(pl.multiple_of(t * DT + i * CR, CR), CR), :]
        result = dot(kvg[my_rows, :], own, ((1,), (1,)))
        for d in range(1, T):
            head = lax.rem(t + d, T)
            result += dot(kvg_tp[head], w2[head, pl.ds(at, CR), :], ((1,), (1,)))
        ig_ref[:, pl.ds(at, CR)] = result.astype(BF)

    loop(NK, igrad)

    loop(NCH * (C - 1), lambda i: w_copy(c, i // (C - 1), lax.rem(i, C - 1) + 1).wait_send())

    def sent_chunk(i):
        owner = i // NCH
        ch = lax.rem(i, NCH)

        @pl.when(owner != c)
        def _():
            sib_copy(owner, ch, lanes).wait_send()

        to, piece = z_target(owner, ch)

        @pl.when(to != t)
        def _():
            z_copy(owner, ch, to, t, piece).wait_send()

    loop(C * NCH, sent_chunk)
    loop(G * C, lambda i: a_copy(i, me).wait_send(), 1)
    loop(G * C, lambda i: p_copy(i, me).wait_send(), 1)
    loop(T, lambda i: t_copy(i, t).wait_send(), 1)
    loop((T - 1) * NK, lambda i: zf_copy(
        lax.rem(t + 1 + i // NK, T), lax.rem(i, NK), lanes).wait_send())

    @pl.when(is_long)
    def _():
        loop(C, lambda to: kv_copy(c, to).wait_send(), c + 1)
        loop(c, lambda owner: d_copy(owner, c).wait_send())


def body(sizes, activations, queries, out_grad, key_weight, value_weight, sessions):
    G, C, T = sizes
    R, D = activations.shape
    WR = key_weight.shape[0]
    QC = queries.shape[1]
    H = QC // HD
    CR = min(WR, 512)
    NCH = WR // CR
    DB = D // (G * C)
    DT = D // T
    NK = DT // CR
    any_ = pl.BlockSpec(memory_space=pl.ANY)
    vmem = pl.BlockSpec(memory_space=pltpu.VMEM)
    dma = pltpu.SemaphoreType.DMA
    V = pltpu.VMEM
    return pl.pallas_call(
        functools.partial(kernel, G, C, T),
        out_shape=(
            jax.ShapeDtypeStruct((R, QC), BF),
            jax.ShapeDtypeStruct((R, QC), BF),
            jax.ShapeDtypeStruct((DB, HD), F32),
            jax.ShapeDtypeStruct((DB, HD), F32),
            jax.ShapeDtypeStruct((R, DT), BF),
        ),
        in_specs=[any_] * 6,
        out_specs=(vmem,) * 5,
        scratch_shapes=[
            V((D, 2 * HD), BF), V((T, DT, 2 * HD), BF), V((R, D), BF), V((R, QC), BF),
            V((R, QC), BF), V((1, R), jnp.int32), V((G * C * R, DB), BF), V((H, R, HD), BF),
            V((H, R, HD), BF), V((C, R, 2 * HD), BF), V((C, H * R, R), F32),
            V((C, R, 2 * HD), F32), V((C, R, 2 * HD), F32),
            V((G * C * R, 2 * HD), BF), V((T, R, 2 * HD), BF),
            V((R, HD), F32), V((R, HD), F32), V((R, 2 * HD), F32), V((H * R, HD), F32),
            dma((6,)),
            dma((C, NCH)), dma((C, NCH)), dma((C, NCH)), dma((C, NCH)),
            dma((C, NCH)), dma((T, NK)), dma((T, NK)), dma((T, NK)),
            dma((G * C,)), dma((G * C,)), dma((C,)), dma((C,)),
            dma((C,)), dma((C,)), dma((G * C,)), dma((G * C,)), dma((T,)), dma((T,)),
        ],
        compiler_params=pltpu.CompilerParams(
            collective_id=0, has_side_effects=True, vmem_limit_bytes=58 * 1024 * 1024
        ),
    )(activations, queries, out_grad, key_weight, value_weight, sessions)


def solution(mesh):
    rows = ("group", "ctx")
    sizes = tuple(mesh.shape[name] for name in ("group", "ctx", "tp"))
    return jax.shard_map(
        functools.partial(body, sizes),
        mesh=mesh,
        in_specs=(
            P(rows, None), P(rows, "tp"), P(rows, "tp"),
            P("ctx", "tp"), P("ctx", "tp"), P("ctx", None),
        ),
        out_specs=(P(rows, "tp"),) * 5,
        check_vma=False,
    )
```

time: 211 us -> 88.4 us (0.42)
  waiting for transfers between devices: 92.4 us -> 0 us
  Pallas kernels: 0 us -> 80.7 us
  blocking collectives: 61.9 us -> 0 us
  matrix products: 16.1 us -> 0 us
  between operations: 14.1 us -> 0.66 us
  other arithmetic: 10.1 us -> 0 us
  local copies, waits for them, and re-layouts: 15.2 us -> 6.89 us
    pallas_call x0 -> x1, Pallas kernels: none -> 80.7 us  [body(): pl.pallas_call(functools.partial(kernel, G, C, T), out_shape=(jax.ShapeDt...]
    all_gather x1 -> x0, waiting for transfers between devices: 53.9 us -> none  [body(): whole_weights = lax.all_gather(both_weights, 'ctx', axis=0, tiled=True)]
    reduce_scatter x2 -> x0, waiting for transfers between devices: 38.5 us -> none  [the longest x1 24.9 us: body(): lax.psum_scatter(key_buffer, 'ctx', scatter_dimension=0, tiled=True)]
    all_gather x2 -> x0, blocking collectives: 31.3 us -> none  [the longest x1 22.4 us: body(): lax.all_gather(kv_grads, ('group', 'ctx'), axis=0, tiled=True)]
    all_to_all x1 -> x0, blocking collectives: 30.6 us -> none  [body(): lax.all_to_all(activations, ('group', 'ctx'), split_axis=1, concat_axis=0...]
    dot_general x10 -> x0, matrix products: 16.1 us -> none  [the longest x1 5.64 us: body(): lax.dot_general(kv_grads, whole_weights, (((1,), (1,)), ((), ())), prefer...]
    concatenate x7 -> x0, other arithmetic: 3.28 us -> none  [the longest x1 2.32 us: body(): both_weights = jnp.concatenate([key_weight, value_weight], 1)]
    all_to_all x1 -> x0, local copies, waits for them, and re-layouts: 2.91 us -> none  [body(): lax.all_to_all(activations, ('group', 'ctx'), split_axis=1, concat_axis=0...]
  transfers between devices with their start and end apart: 3 -> 0, of which waited for: 3 -> 0; matrix products, arithmetic and copies ran while one was open for 6% -> 0% of each run, Pallas kernels for 0% -> 0%
where the time goes in v1:
time: 88.4 us; the launch traced here: 88.2 us
  Pallas kernels  80.7 us (91%)
  local copies, waits for them, and re-layouts  6.89 us (8%)
    pallas_call x1, Pallas kernels, body(): pl.pallas_call(functools.partial(kernel, G, C, T), out_shape=(jax.ShapeDt...  80.7 us
    unnamed x9, local copies, waits for them, and re-layouts  6.89 us

profile of v1, /device:TPU:0, one launch (start us, length us, event | category | flops | bytes accessed | tf_op | source)
XLA Modules:
  0.0 88.2 jit_solution(16295821611983725354)
XLA Ops:
  0.6 80.7 %shard_map.101 = (bf16[128,1024]{1,0:T(8,128)(2,1)}, bf16[128,1024]{1,0:T(8,128)(2,1)}, f32[1024,128]{1,0:T(8,128)}, f32[1024,128]{1,0:T(8,128)}, bf16[128,2048]{1,0:T(8,128)(2,1)}) custom-call(bf16[128,8192]{1,0:T(8,128)(2,1)} %act_hbm.1, bf16[128,1024]{1,0:T(8,128)(2,1)} %q_hbm.1, bf16[128,1024]{1,0:T(8,128)(2,1)} %do_hbm.1, bf16[2048,128]{1,0:T(8,128)(2,1)} %wk_hbm.1, ...), custom_call_target="tpu_custom_call" | custom-call | tf_op jit(solution)/shard_map/pallas_call | solution.py:399
  81.3 0.0 copy-start.1
  81.3 0.0 copy-start
  81.3 1.8 %copy.16 = bf16[128,1024]{1,0:T(8,128)(2,1)} copy(bf16[128,1024]{1,0:T(8,128)(2,1)} %get-tuple-element.10) | data formatting | bytes 524288
  83.1 1.7 %copy.17 = bf16[128,1024]{1,0:T(8,128)(2,1)} copy(bf16[128,1024]{1,0:T(8,128)(2,1)} %get-tuple-element.11) | data formatting | bytes 524288
  84.7 1.9 %copy.18 = f32[1024,128]{1,0:T(8,128)} copy(f32[1024,128]{1,0:T(8,128)} %get-tuple-element.12) | data formatting | bytes 1048576
  86.6 0.0 copy-done.1
  86.6 0.8 copy.19
  87.4 0.0 copy-done
  87.4 0.8 copy.20
Async XLA Ops:
  81.3 5.3 %copy-start.1 = (f32[1024,128]{1,0:T(8,128)S(1)}, f32[1024,128]{1,0:T(8,128)}, u32[]{:S(2)}) copy-start(f32[1024,128]{1,0:T(8,128)} %get-tuple-element.13) | copy-start | bytes 1572868
  81.3 6.1 %copy-start = (bf16[128,2048]{1,0:T(8,128)(2,1)S(1)}, bf16[128,2048]{1,0:T(8,128)(2,1)}, u32[]{:S(2)}) copy-start(bf16[128,2048]{1,0:T(8,128)(2,1)} %get-tuple-element.14) | copy-start | bytes 1572868

commit v2 on v1

--- a/solution.py
+++ b/solution.py
@@ -193,7 +193,6 @@
     def a_start(i):
         a_copy(i, me).start()
 
-    loop(G * C, a_start, 1)
     own_a = pltpu.make_async_copy(
         act.at[:, pl.ds(pl.multiple_of(me * DB, DB), DB)],
         arecv.at[pl.ds(pl.multiple_of(me * R, R), R), :],
@@ -234,6 +233,7 @@
 
     count = c + 1 - first_block
     top = lax.fori_loop(0, count, score_pass, jnp.full((H * R, 1), -jnp.inf, F32))
+    loop(G * C // 2, a_start, 1)
 
     def sum_pass(j, total):
         return total + jnp.sum(jnp.exp(scores[j] - top), 1, keepdims=True)
@@ -273,6 +273,7 @@
         dq_acc[...] += dot(ds, kv[j, :, :HD], ((1,), (0,)))
 
     loop(c + 1, grad_pass, first_block)
+    loop(G * C, a_start, G * C // 2)
     for h in range(H):
         turned = rope(dq_acc[h * R:(h + 1) * R] * scale, -1.0)
         dq_ref[:, h * HD:(h + 1) * HD] = turned.astype(BF)
@@ -315,24 +316,6 @@
         zf_copy(head, piece, lanes).start()
 
     loop((T - 1) * NK, z_arrived)
-
-    own_a.wait()
-
-    def a_wait(i):
-        slot = lax.rem(me + i, G * C)
-        a_copy(0, slot).wait_recv()
-        p_copy(0, slot).wait_recv()
-
-    loop(G * C, a_wait, 1)
-    step = min(DB, 256)
-
-    def wgrad(i):
-        at = pl.ds(pl.multiple_of(i * step, step), step)
-        both = dot(arecv[:, at], kvg[...], ((0,), (0,)))
-        kwg_ref[at, :] = both[:, :HD]
-        vwg_ref[at, :] = both[:, HD:]
-
-    loop(DB // step, wgrad)
 
     loop(T, lambda i: t_copy(0, lax.rem(t + i, T)).wait_recv(), 1)
 
@@ -352,6 +335,24 @@
 
     loop(NK, igrad)
 
+    own_a.wait()
+
+    def a_wait(i):
+        slot = lax.rem(me + i, G * C)
+        a_copy(0, slot).wait_recv()
+        p_copy(0, slot).wait_recv()
+
+    loop(G * C, a_wait, 1)
+    step = min(DB, 256)
+
+    def wgrad(i):
+        at = pl.ds(pl.multiple_of(i * step, step), step)
+        both = dot(arecv[:, at], kvg[...], ((0,), (0,)))
+        kwg_ref[at, :] = both[:, :HD]
+        vwg_ref[at, :] = both[:, HD:]
+
+    loop(DB // step, wgrad)
+
     loop(NCH * (C - 1), lambda i: w_copy(c, i // (C - 1), lax.rem(i, C - 1) + 1).wait_send())
 
     def sent_chunk(i):
@@ -379,6 +380,32 @@
     def _():
         loop(C, lambda to: kv_copy(c, to).wait_send(), c + 1)
         loop(c, lambda owner: d_copy(owner, c).wait_send())
+
+
+def copy_kernel(n, *refs):
+    sems = refs[2 * n]
+    hold = refs[2 * n + 1:]
+    come = [pltpu.make_async_copy(refs[k], hold[k], sems.at[k]) for k in range(n)]
+    leave = [pltpu.make_async_copy(hold[k], refs[n + k], sems.at[n + k]) for k in range(n)]
+    for one in come:
+        one.start()
+    for k in range(n):
+        come[k].wait()
+        leave[k].start()
+    for one in leave:
+        one.wait()
+
+
+def hand_out(arrays):
+    n = len(arrays)
+    any_ = pl.BlockSpec(memory_space=pl.ANY)
+    return pl.pallas_call(
+        functools.partial(copy_kernel, n),
+        out_shape=tuple(jax.ShapeDtypeStruct(a.shape, a.dtype) for a in arrays),
+        in_specs=[any_] * n,
+        out_specs=(any_,) * n,
+        scratch_shapes=[pltpu.SemaphoreType.DMA((2 * n,))] + [pltpu.VMEM(a.shape, a.dtype) for a in arrays],
+    )(*arrays)
 
 
 def body(sizes, activations, queries, out_grad, key_weight, value_weight, sessions):
@@ -396,7 +423,7 @@
     vmem = pl.BlockSpec(memory_space=pltpu.VMEM)
     dma = pltpu.SemaphoreType.DMA
     V = pltpu.VMEM
-    return pl.pallas_call(
+    made = pl.pallas_call(
         functools.partial(kernel, G, C, T),
         out_shape=(
             jax.ShapeDtypeStruct((R, QC), BF),
@@ -424,6 +451,7 @@
             collective_id=0, has_side_effects=True, vmem_limit_bytes=58 * 1024 * 1024
         ),
     )(activations, queries, out_grad, key_weight, value_weight, sessions)
+    return hand_out(made)
 
 
 def solution(mesh):

time: 88.4 us -> 73.7 us (0.83)
  Pallas kernels: 80.7 us -> 73 us
  local copies, waits for them, and re-layouts: 6.89 us -> 0 us
    pallas_call x1, Pallas kernels: 80.7 us -> 70.5 us  [body(): pl.pallas_call(functools.partial(kernel, G, C, T), out_shape=(jax.ShapeDt...]
    unnamed x9 -> x0, local copies, waits for them, and re-layouts: 6.89 us -> none
    pallas_call x0 -> x1, Pallas kernels: none -> 2.43 us  [hand_out(): pl.pallas_call(functools.partial(copy_kernel, n), out_shape=tuple((jax.Sh...]
where the time goes in v2:
time: 73.7 us; the launch traced here: 73.6 us
  Pallas kernels  73 us (99%)
    pallas_call x1, Pallas kernels, body(): pl.pallas_call(functools.partial(kernel, G, C, T), out_shape=(jax.ShapeDt...  70.5 us
    pallas_call x1, Pallas kernels, hand_out(): pl.pallas_call(functools.partial(copy_kernel, n), out_shape=tuple((jax.Sh...  2.43 us

profile of v2, /device:TPU:0, one launch (start us, length us, event | category | flops | bytes accessed | tf_op | source)
XLA Modules:
  0.0 73.6 jit_solution(10054371832236379918)
XLA Ops:
  0.6 70.5 %shard_map.101 = (bf16[128,1024]{1,0:T(8,128)(2,1)}, bf16[128,1024]{1,0:T(8,128)(2,1)}, f32[1024,128]{1,0:T(8,128)}, f32[1024,128]{1,0:T(8,128)}, bf16[128,2048]{1,0:T(8,128)(2,1)}) custom-call(bf16[128,8192]{1,0:T(8,128)(2,1)} %act_hbm.1, bf16[128,1024]{1,0:T(8,128)(2,1)} %q_hbm.1, bf16[128,1024]{1,0:T(8,128)(2,1)} %do_hbm.1, bf16[2048,128]{1,0:T(8,128)(2,1)} %wk_hbm.1, ...), custom_call_target="tpu_custom_call" | custom-call | tf_op jit(solution)/shard_map/pallas_call | solution.py:426
  71.2 2.4 %shard_map.102 = (bf16[128,1024]{1,0:T(8,128)(2,1)}, bf16[128,1024]{1,0:T(8,128)(2,1)}, f32[1024,128]{1,0:T(8,128)}, f32[1024,128]{1,0:T(8,128)}, bf16[128,2048]{1,0:T(8,128)(2,1)}) custom-call(bf16[128,1024]{1,0:T(8,128)(2,1)} %get-tuple-element.10.refs_0_, bf16[128,1024]{1,0:T(8,128)(2,1)} %get-tuple-element.11.refs_1_, ...), custom_call_target="tpu_custom_call" | custom-call | tf_op jit(solution)/shard_map/pallas_call | solution.py:402

commit v3 on v2

--- a/solution.py
+++ b/solution.py
@@ -101,7 +101,26 @@
     def send_w(i):
         w_copy(c, i // (C - 1), lax.rem(i, C - 1) + 1).start()
 
-    loop(NCH * (C - 1), send_w)
+    square = C == 4
+    beside = c + 1 - 2 * lax.rem(c, 2)
+    across = lax.rem(c + 2, C)
+    corner = C - 1 - c
+
+    def near_copy(owner, ch, d, to):
+        place = wall.at[rows_of(owner, ch), lanes]
+        return remote(place, place, w_s.at[d, ch], w_r.at[owner, ch], ctx=to)
+
+    def relay_copy(ch):
+        if ch % 2:
+            return near_copy(beside, ch, 3, across)
+        return near_copy(across, ch, 3, beside)
+
+    if square:
+        for ch in range(NCH):
+            near_copy(c, ch, 1, beside).start()
+            near_copy(c, ch, 2, across).start()
+    else:
+        loop(NCH * (C - 1), send_w)
 
     def sib_copy(owner, ch, which):
         place = wall.at[rows_of(owner, ch), which]
@@ -172,6 +191,12 @@
         sib_copy(owner, ch, olanes).wait_recv()
         project(owner, ch)
 
+    order = []
+    for ch in range(NCH + 1):
+        near = [(beside, ch, ch % 2 == 1), (across, ch, ch % 2 == 0)] if ch < NCH else []
+        far = [(corner, ch - 1, False)] if ch > 0 else []
+        order.append(near + far)
+
     def chunk(ch):
         loop((ch + 1) * (C - 1), arrived, ch * (C - 1))
 
@@ -179,7 +204,23 @@
         def _():
             loop(ch * (C - 1), use, (ch - 1) * (C - 1))
 
-    loop(NCH, chunk)
+    def take(owner, ch):
+        sib_copy(owner, ch, olanes).wait_recv()
+        project(owner, ch)
+
+    if square:
+        for k, now in enumerate(order):
+            for owner, ch, relay in now:
+                w_copy(owner, ch, 1).wait_recv()
+                if relay:
+                    relay_copy(ch).start()
+                sib_copy(owner, ch, lanes).start()
+                z_start(owner, ch)
+            if k > 0:
+                for owner, ch, relay in order[k - 1]:
+                    take(owner, ch)
+    else:
+        loop(NCH, chunk)
 
     def a_copy(i, slot):
         b = lax.rem(me + i, G * C)
@@ -199,7 +240,11 @@
         loc.at[0],
     )
     own_a.start()
-    loop(NCH * (C - 1), use, (NCH - 1) * (C - 1))
+    if square:
+        for owner, ch, relay in order[NCH]:
+            take(owner, ch)
+    else:
+        loop(NCH * (C - 1), use, (NCH - 1) * (C - 1))
 
     kv[c, :, :HD] = rope(proj[:, :HD], 1.0).astype(BF)
     kv[c, :, HD:] = proj[:, HD:].astype(BF)
@@ -353,7 +398,13 @@
 
     loop(DB // step, wgrad)
 
-    loop(NCH * (C - 1), lambda i: w_copy(c, i // (C - 1), lax.rem(i, C - 1) + 1).wait_send())
+    if square:
+        for ch in range(NCH):
+            near_copy(c, ch, 1, beside).wait_send()
+            near_copy(c, ch, 2, across).wait_send()
+            relay_copy(ch).wait_send()
+    else:
+        loop(NCH * (C - 1), lambda i: w_copy(c, i // (C - 1), lax.rem(i, C - 1) + 1).wait_send())
 
     def sent_chunk(i):
         owner = i // NCH

time: 73.7 us -> 72.1 us (0.978)
  the two profiles are of different devices: /device:TPU:0 before, /device:TPU:13 now
where the time goes in v3:
time: 72.1 us; the launch traced here: 72 us
  Pallas kernels  71.3 us (99%)
    pallas_call x1, Pallas kernels, body(): pl.pallas_call(functools.partial(kernel, G, C, T), out_shape=(jax.ShapeDt...  68.9 us
    pallas_call x1, Pallas kernels, hand_out(): pl.pallas_call(functools.partial(copy_kernel, n), out_shape=tuple((jax.Sh...  2.43 us

profile of v3, /device:TPU:13, one launch (start us, length us, event | category | flops | bytes accessed | tf_op | source)
XLA Modules:
  0.0 72.0 jit_solution(11953545585917097276)
XLA Ops:
  0.6 68.9 %shard_map.101 = (bf16[128,1024]{1,0:T(8,128)(2,1)}, bf16[128,1024]{1,0:T(8,128)(2,1)}, f32[1024,128]{1,0:T(8,128)}, f32[1024,128]{1,0:T(8,128)}, bf16[128,2048]{1,0:T(8,128)(2,1)}) custom-call(bf16[128,8192]{1,0:T(8,128)(2,1)} %act_hbm.1, bf16[128,1024]{1,0:T(8,128)(2,1)} %q_hbm.1, bf16[128,1024]{1,0:T(8,128)(2,1)} %do_hbm.1, bf16[2048,128]{1,0:T(8,128)(2,1)} %wk_hbm.1, ...), custom_call_target="tpu_custom_call" | custom-call | tf_op jit(solution)/shard_map/pallas_call | solution.py:477
  69.5 2.4 %shard_map.102 = (bf16[128,1024]{1,0:T(8,128)(2,1)}, bf16[128,1024]{1,0:T(8,128)(2,1)}, f32[1024,128]{1,0:T(8,128)}, f32[1024,128]{1,0:T(8,128)}, bf16[128,2048]{1,0:T(8,128)(2,1)}) custom-call(bf16[128,1024]{1,0:T(8,128)(2,1)} %get-tuple-element.10.refs_0_, bf16[128,1024]{1,0:T(8,128)(2,1)} %get-tuple-element.11.refs_1_, ...), custom_call_target="tpu_custom_call" | custom-call | tf_op jit(solution)/shard_map/pallas_call | solution.py:453
